TPU v7x, 512 devices: a whole 4x8x8 slice. The times are simulated.
512 devices in a mesh: gr: 16 (over y, core), gc: 8 (over z), hd: 4 (over x).
Axes of the slice: x: 4, y: 8, z: 8, core: 2. Of those that a mesh axis runs over, the one named last changes fastest.
Arguments:
- patches: bfloat16 [128, 64, 1024], P('gr', 'gc', 'hd'), may hold values from -6 to 6
- w_in: bfloat16 [1024, 2, 1024], P(None, None, 'hd'), may hold values from -0.1875 to 0.1875
- w_bc: bfloat16 [1024, 4, 64], replicated, may hold values from -0.0625 to 0.0625
- w_step: bfloat16 [1024, 2, 16], P(None, None, 'hd'), may hold values from -0.1875 to 0.1875
- step_bias: float32 [2, 16], P(None, 'hd'), may hold values from -3 to 0.5
- decay_rate: float32 [2, 16], P(None, 'hd'), may hold values from 0.004 to 0.08
- skip_gain: float32 [16], P('hd'), may hold values from 0.25 to 2
- norm_gain: float32 [1024], P('hd'), may hold values from 0.25 to 1.75
- w_out: bfloat16 [1024, 1024], P('hd'), may hold values from -0.25 to 0.25
Outputs:
- mixed: bfloat16 [128, 64, 1024], P('gr', 'gc', 'hd')
All inputs are finite; a program needn't handle non-finite values.
Results may differ from a plain program's by a relative error of at most 0.0049.
Values may be sent and summed in bfloat16 or wider, within the bound.
A program may use at most 64 MiB of HBM per device.

v0:
```python
import jax
import jax.numpy as jnp
from jax import lax
from jax.sharding import PartitionSpec as P


def carried_in(shard, axis, combine, identity):
    length, index = (lax.axis_size(axis), lax.axis_index(axis))
    everything = jax.tree.map(lambda part: lax.all_gather(part, axis), shard)
    start = jax.tree.map(
        lambda part, zero: jnp.broadcast_to(jnp.asarray(zero, part.dtype), part.shape),
        shard,
        identity,
    )

    def step(k, before):
        reached = k < index
        new = combine(before, jax.tree.map(lambda part: part[k], everything))
        return jax.tree.map(lambda a, b: jnp.where(reached, a, b), new, before)

    return lax.fori_loop(0, length, step, start)


def tile_terms(rates, bmat, cmat, inputs):
    cum = jnp.cumsum(rates, axis=1)
    length = rates.shape[1]
    diff = cum[:, :, None, :] - cum[:, None, :, :]
    lower = lax.broadcasted_iota(jnp.int32, (length, length), 0) >= lax.broadcasted_iota(
        jnp.int32, (length, length), 1
    )
    weights = jnp.exp(jnp.where(lower[None, :, :, None], diff, -1e30))
    scores = jnp.einsum("acn,ajn->acj", cmat, bmat, precision=lax.Precision.HIGHEST)
    mixing = scores[:, :, :, None] * weights
    within = jnp.einsum("acjh,ajhp->achp", mixing, inputs, precision=lax.Precision.HIGHEST)
    last = cum[:, -1, :]
    tail = jnp.exp(last[:, None, :] - cum)
    state = jnp.einsum("ajh,ajn,ajhp->ahnp", tail, bmat, inputs, precision=lax.Precision.HIGHEST)
    return (cum, within, last, state)


def apply_carry(within, cum, cmat, incoming):
    readout = jnp.einsum("acn,ahnp->achp", cmat, incoming, precision=lax.Precision.HIGHEST)
    return within + jnp.exp(cum)[..., None] * readout


def combine(earlier, later):
    return (earlier[0] + later[0], jnp.exp(later[0])[:, :, None, None] * earlier[1] + later[1])


def on_device(patches, w_in, w_bc, w_step, step_bias, decay_rate, skip_gain, norm_gain, w_out):
    full = lax.all_gather(patches, "hd", axis=2, tiled=True)
    rows, cols, width = full.shape
    heads = w_step.shape[2]
    inner_width = w_in.shape[2]
    hsize = inner_width // heads
    flat = full.reshape(rows * cols, width)
    inner = jnp.dot(flat, w_in.reshape(width, 2 * inner_width), preferred_element_type=jnp.float32)
    inner = inner.reshape(rows, cols, 2, heads, hsize)
    uvals = inner[:, :, 0]
    gate = inner[:, :, 1]
    bc = jnp.dot(flat, w_bc.reshape(width, -1), preferred_element_type=jnp.float32).reshape(
        rows, cols, 4, -1
    )
    raw = jnp.dot(
        flat, w_step.reshape(width, 2 * heads), preferred_element_type=jnp.float32
    ).reshape(rows, cols, 2, heads)
    steps = jax.nn.softplus(raw + step_bias)
    rates = -decay_rate * steps
    hcum, hwithin, hlast, hstate = tile_terms(
        rates[:, :, 0], bc[:, :, 0], bc[:, :, 1], steps[:, :, 0, :, None] * uvals
    )
    hpair = (hlast, hstate)
    hzero = (jnp.zeros_like(hlast), jnp.zeros_like(hstate))
    hin = carried_in(hpair, "gc", combine, hzero)[1]
    yh = apply_carry(hwithin, hcum, bc[:, :, 1], hin) + skip_gain[:, None] * uvals
    vrates = rates[:, :, 1].transpose(1, 0, 2)
    vbmat = bc[:, :, 2].transpose(1, 0, 2)
    vcmat = bc[:, :, 3].transpose(1, 0, 2)
    vinput = (steps[:, :, 1, :, None] * yh).transpose(1, 0, 2, 3)
    vcum, vwithin, vlast, vstate = tile_terms(vrates, vbmat, vcmat, vinput)
    vpair = (vlast, vstate)
    vzero = (jnp.zeros_like(vlast), jnp.zeros_like(vstate))
    vin = carried_in(vpair, "gr", combine, vzero)[1]
    yv = apply_carry(vwithin, vcum, vcmat, vin).transpose(1, 0, 2, 3) + yh
    meansq = jnp.mean(yv * yv, axis=-1, keepdims=True)
    normed = yv * lax.rsqrt(meansq + 1e-05) * norm_gain.reshape(heads, hsize)
    hidden = (normed * jax.nn.silu(gate)).astype(jnp.bfloat16).reshape(rows * cols, inner_width)
    partial_out = jnp.dot(hidden, w_out, preferred_element_type=jnp.float32).reshape(
        rows, cols, w_out.shape[1]
    )
    return lax.psum_scatter(partial_out, "hd", scatter_dimension=2, tiled=True).astype(jnp.bfloat16)


def solution(mesh):
    in_specs = (
        P("gr", "gc", "hd"),
        P(None, None, "hd"),
        P(),
        P(None, None, "hd"),
        P(None, "hd"),
        P(None, "hd"),
        P("hd"),
        P("hd"),
        P("hd", None),
    )
    out_specs = P("gr", "gc", "hd")
    return jax.shard_map(
        on_device, mesh=mesh, in_specs=in_specs, out_specs=out_specs, check_vma=False
    )
```

profile of v0, /device:TPU:1, one launch (start us, length us, event | category | flops | bytes accessed | tf_op | source)
XLA Modules:
  0.0 304.1 jit_solution(1298587718123060350)
XLA Ops:
  6.5 0.7 neg.12
  7.3 0.7 reshape.75
  8.0 10.5 %all_gather.21 = bf16[8,8,1024]{2,1,0:T(8,128)(2,1)S(1)} all-gather(bf16[8,8,256]{2,1,0:T(8,128)(2,1)} %param.13), channel_id=1, replica_groups=mesh['gr'=16,'gc'=8,'hd'=4] {'hd'}, dimensions={2}, use_global_device_ids=true | all-gather | bytes 163840 | tf_op jit(solution)/shard_map/all_gather | solution.py:51
  18.5 1.1 broadcast_multiply_fusion
  19.7 1.4 reduce_window_sum.17
  21.5 1.4 fusion.4
  22.9 1.4 copy.81
  24.3 0.5 copy.48
  24.9 0.6 fusion.8
  25.5 3.0 fusion.21
  28.8 24.5 %all-gather = f32[64,1,4]{2,1,0:T(1,128)S(1)} all-gather(f32[8,1,4]{2,1,0:T(1,128)S(1)} %copy.50), channel_id=2, replica_groups=mesh['gr'=16,'gc'=8,'hd'=4] {'gc'}, dimensions={0}, use_global_device_ids=true | all-gather | bytes 1152 | tf_op jit(solution)/shard_map/all_gather | solution.py:9
  53.6 79.7 %all-gather.7.cloned.1.call-done = f32[64,4,64,64]{3,2,1,0:T(8,128)} async-done(((f32[8,4,64,64]{3,2,1,0:T(8,128)}), f32[64,4,64,64]{3,2,1,0:T(8,128)}) %all-gather.7.cloned.1.call-update) | async-done | bytes 4194320 | tf_op jit(solution)/shard_map/all_gather | solution.py:9
  133.3 12.6 %while.28 = (s32[]{:T(128)}, f32[8,4,64,64]{3,2,1,0:T(8,128)S(1)}, s32[]{:T(128)}, f32[8,8,4]{1,2,0:T(4,128)S(1)}, f32[8,8,4,64,64]{4,3,2,1,0:T(8,128)}, /*index=5*/s32[]{:T(128)}, s32[]{:T(128)}) while((s32[]{:T(128)}, f32[8,4,64,64]{3,2,1,0:T(8,128)S(1)}, s32[]{:T(128)}, f32[8,8,4]{1,2,0:T(4,128)S(1)}, ...), condition=%wide.region_2.3_spmd.clone, body=%wide.region_1.2_spmd.clone.sunk | while | flops 524292 | bytes 1573617 | solution.py:21
  133.4 1.5 fusion.72
  135.0 1.5 fusion.72
  136.5 1.5 fusion.72
  138.1 1.5 fusion.72
  139.7 1.5 fusion.72
  141.3 1.5 fusion.72
  142.9 1.5 fusion.72
  144.5 1.5 fusion.72
  145.9 0.6 convolution_multiply_fusion
  146.6 0.4 fusion.3
  147.1 2.9 fusion.14
  150.3 17.6 %all-gather.2 = f32[128,1,4]{2,1,0:T(1,128)S(1)} all-gather(f32[8,1,4]{2,1,0:T(1,128)S(1)} %copy.61), channel_id=4, replica_groups=mesh['gr'=16,'gc'=8,'hd'=4] {'gr'}, dimensions={0}, use_global_device_ids=true | all-gather | bytes 2176 | tf_op jit(solution)/shard_map/all_gather | solution.py:9
  168.2 0.4 fusion.16
  168.7 77.6 %all-gather.9.cloned.1.call-done = f32[128,4,64,64]{3,2,1,0:T(8,128)} async-done(((f32[8,4,64,64]{3,2,1,0:T(8,128)}), f32[128,4,64,64]{3,2,1,0:T(8,128)}) %all-gather.9.cloned.1.call-update) | async-done | bytes 8388624 | tf_op jit(solution)/shard_map/all_gather | solution.py:9
  246.3 25.3 %while.29 = (s32[]{:T(128)}, f32[8,4,64,64]{3,2,1,0:T(8,128)S(1)}, s32[]{:T(128)}, f32[16,8,4]{1,2,0:T(4,128)S(1)}, f32[16,8,4,64,64]{4,3,2,1,0:T(8,128)}, /*index=5*/s32[]{:T(128)}, s32[]{:T(128)}) while((s32[]{:T(128)}, f32[8,4,64,64]{3,2,1,0:T(8,128)S(1)}, s32[]{:T(128)}, f32[16,8,4]{1,2,0:T(4,128)S(1)}, ...), condition=%wide.region_5.6_spmd.clone, body=%wide.region_4.5_spmd.clone.sunk | while | flops 524292 | bytes 1573617 | solution.py:21
  246.4 1.5 fusion.73
  248.0 1.5 fusion.73
  249.6 1.5 fusion.73
  251.2 1.5 fusion.73
  252.8 1.5 fusion.73
  254.3 1.5 fusion.73
  255.9 1.5 fusion.73
  257.5 1.5 fusion.73
  259.1 1.5 fusion.73
  260.7 1.5 fusion.73
  262.3 1.5 fusion.73
  263.8 1.5 fusion.73
  265.4 1.5 fusion.73
  267.0 1.5 fusion.73
  268.6 1.5 fusion.73
  270.2 1.5 fusion.73
  271.6 0.6 fusion.49
  272.8 0.9 fusion.6
  273.7 22.4 %reduce-scatter.2.cloned.1.call-done = f32[8,8,256]{2,1,0:T(8,128)} async-done(((f32[8,8,1024]{2,1,0:T(8,128)}), f32[8,8,256]{2,1,0:T(8,128)}) %reduce-scatter.2.cloned.1.call-update) | async-done | bytes 65552 | tf_op jit(solution)/shard_map/reduce_scatter | solution.py:91
  296.1 1.5 convert_element_type.7
  (89 shorter events, 4.5 us)
Async XLA Ops:
  6.5 266.3 %copy-start = (bf16[256,1024]{1,0:T(8,128)(2,1)S(1)}, bf16[256,1024]{1,0:T(8,128)(2,1)}, u32[]{:S(2)}) copy-start(bf16[256,1024]{1,0:T(8,128)(2,1)} %param.21) | copy-start | bytes 1572868
  6.5 140.0 %copy-start.2 = (f32[4]{0:T(128)S(1)}, f32[4]{0:T(128)}, u32[]{:S(2)}) copy-start(f32[4]{0:T(128)} %param.19) | copy-start | bytes 52
  6.5 143.6 %copy-start.1 = (f32[256]{0:T(256)S(1)}, f32[256]{0:T(256)}, u32[]{:S(2)}) copy-start(f32[256]{0:T(256)} %param.20) | copy-start | bytes 3076
  6.5 126.7 %all-gather.7.cloned.1.call-start = ((), (), s32[]{:S(2)}) async-start(), calls=%async_computation.2 | async-start | bytes 9437184 | tf_op jit(solution)/shard_map/all_gather | solution.py:9
  28.5 217.8 %all-gather.9.cloned.1.call-start = ((), (), s32[]{:S(2)}) async-start(), calls=%async_computation.3 | async-start | bytes 17825792 | tf_op jit(solution)/shard_map/all_gather | solution.py:9
  150.0 146.2 %reduce-scatter.2.cloned.1.call-start = ((), (), s32[]{:S(2)}) async-start(), calls=%async_computation.1 | async-start | bytes 327680 | tf_op jit(solution)/shard_map/reduce_scatter | solution.py:91
Sparse Core Ops, SparseCore 0:
  28.6 104.6 all-gather.6
  150.1 96.1 all-gather.8
  273.9 22.2 reduce-scatter.1
where the time goes:
time: 307 us; the launch traced here: 304 us
  waiting for transfers between devices  180 us (59%)
  blocking collectives  52.6 us (17%)
  other arithmetic  39.2 us (13%)
  between operations  13.3 us (4%)
  matrix products  12.4 us (4%)
  local copies, waits for them, and re-layouts  6.1 us (2%)
    all_gather x2, waiting for transfers between devices, carried_in(): everything = jax.tree.map(lambda part: lax.all_gather(part, axis), shard)  157 us
    all_gather x2, blocking collectives, carried_in(): everything = jax.tree.map(lambda part: lax.all_gather(part, axis), shard)  42.1 us
    select_n x24, other arithmetic, step(): return jax.tree.map(lambda a, b: jnp.where(reached, a, b), new, before)  35 us
    reduce_scatter x1, waiting for transfers between devices, on_device(): lax.psum_scatter(partial_out, 'hd', scatter_dimension=2, tiled=True)  22.4 us
    all_gather x1, blocking collectives, on_device(): full = lax.all_gather(patches, 'hd', axis=2, tiled=True)  10.5 us
  transfers between devices with their start and end apart: 3, of which 3 were waited for; matrix products, arithmetic and copies ran while one was open for 1% of the time, Pallas kernels for 0%

commit v1 on v0

v1 whole, which is shorter than its diff:
```python
import functools

import jax
import jax.numpy as jnp
from jax import lax
from jax.experimental import pallas as pl
from jax.experimental.pallas import tpu as pltpu
from jax.sharding import PartitionSpec as P

MESH = pl.DeviceIdType.MESH
F32, BF16 = jnp.float32, jnp.bfloat16
FAR_FIRST_8 = (4, 3, 5, 2, 6, 1, 7)
FAR_FIRST_4 = (2, 1, 3)


def nn(a, b):
    return lax.dot_general(a, b, (((1,), (0,)), ((), ())), preferred_element_type=F32)


def nt(a, b):
    return lax.dot_general(a, b, (((1,), (1,)), ((), ())), preferred_element_type=F32)


def split(a):
    high = a.astype(BF16)
    return high, (a - high.astype(F32)).astype(BF16)


def iotas(shape):
    return lax.broadcasted_iota(jnp.int32, shape, 0), lax.broadcasted_iota(jnp.int32, shape, 1)


def by_head(values, shape):
    lane = lax.broadcasted_iota(jnp.int32, shape, 1)
    row = jnp.full(shape, values[-1], F32)
    for h in range(len(values) - 2, -1, -1):
        row = jnp.where(lane < 64 * (h + 1), values[h], row)
    return row


def dots(c, b, copies):
    (c_high, c_low), (b_high, b_low) = split(c), split(b)
    lane = iotas(c.shape)[1]
    zero = jnp.zeros((), BF16)
    left = [jnp.where(lane < 64, c_high, c_low), jnp.where(lane < 64, c_high, zero)]
    right = jnp.concatenate([b_high, jnp.where(lane < 64, b_low, zero)], axis=1)
    return nt(jnp.concatenate(left, axis=1), jnp.concatenate([right] * copies, axis=0))


def segment_sums(rates, length, heads):
    k, lane = iotas((length, heads * length))
    inside = jnp.where(k > lane % length, rates, 0.0)
    high, low = split(inside)
    i, j = iotas((length, 2 * length))
    lower = jnp.where(i >= j % length, 1.0, 0.0).astype(BF16)
    return nn(lower, jnp.concatenate([high, low], axis=0))


def layer(
    patches, w_in, w_bc, w_step, bias_in, decay_in, skip_in, gain_in, w_out, out,
    pt, zs, zb, xr, xt, wi, wd, wb, wst, wh, wv, woc, gain, bias, decay, skip,
    yhz, yhb, es, eb, ys, yb, hs, hb, hx, ot, mix,
    load_sem, send_sem, recv_sem,
):
    gr, gc, hd = lax.axis_index("gr"), lax.axis_index("gc"), lax.axis_index("hd")
    chip, core = lax.div(gr, 2), lax.rem(gr, 2)

    x_peers = [lax.rem(hd + k, 4) for k in FAR_FIRST_4]
    z_peers = [lax.rem(gc + k, 8) for k in FAR_FIRST_8]
    y_peers = [2 * lax.rem(chip + k, 8) + c for k in FAR_FIRST_8 for c in (core, 1 - core)]
    y_peers.append(2 * chip + 1 - core)

    barrier = pltpu.get_barrier_semaphore()
    for p in z_peers:
        pl.semaphore_signal(barrier, inc=1, device_id=(gr, p, hd), device_id_type=MESH)
    for p in y_peers:
        pl.semaphore_signal(barrier, inc=1, device_id=(p, gc, hd), device_id_type=MESH)
    for p in x_peers:
        pl.semaphore_signal(barrier, inc=1, device_id=(gr, gc, p), device_id_type=MESH)

    def columns(p):
        return w_out.at[:, pl.ds(pl.multiple_of(p * 256, 256), 256)]

    loads = [
        pltpu.make_async_copy(src, dst, load_sem.at[n])
        for n, (src, dst) in enumerate(
            (
                (patches, pt),
                (w_step, wst),
                (w_bc, wb),
                (w_in, wi),
                (bias_in, bias),
                (decay_in, decay),
                (skip_in, skip),
                (gain_in, gain),
                (columns(hd), woc.at[hd]),
            )
        )
    ]
    for load in loads:
        load.start()

    def send(phase, src, dst, device):
        pltpu.make_async_remote_copy(
            src_ref=src,
            dst_ref=dst,
            send_sem=send_sem.at[phase],
            recv_sem=recv_sem.at[phase],
            device_id=device,
            device_id_type=MESH,
        ).start()

    def whole(phase, buf):
        part = buf.at[:, pl.ds(0, 56), :] if phase == 4 else buf.at[pl.ds(0, buf.shape[0] - 1)]
        return pltpu.make_async_remote_copy(
            src_ref=part,
            dst_ref=part,
            send_sem=send_sem.at[phase],
            recv_sem=recv_sem.at[phase],
            device_id=(gr, gc, x_peers[0]),
            device_id_type=MESH,
        )

    loads[0].wait()
    tile = pt[...].astype(F32)
    for r in range(8):
        zs[r] = jnp.concatenate([tile[r, :, 0:128], tile[r, :, 128:256]], axis=0).astype(BF16)
        for half in range(2):
            ot[half, 8 * r : 8 * r + 8, :] = tile[r, :, 128 * half : 128 * half + 128]
    for c in range(0, 8, 2):
        for half in range(2):
            pair = [ot[half, pl.ds(c + d, 8, stride=8), :] for d in (0, 1)]
            xt[hd, 8 * c : 8 * c + 16, 128 * half : 128 * half + 128] = jnp.concatenate(
                pair, axis=0
            ).astype(BF16)
    zb[gc] = zs[gc]

    pl.semaphore_wait(barrier, 25)

    for p in z_peers:
        send(0, zs.at[p], zb.at[gc], (gr, p, hd))
    for p in x_peers:
        send(1, xt.at[hd], xt.at[hd], (gr, gc, p))

    for load in loads[1:]:
        load.wait()

    def pairs(n, carry):
        rows = pl.ds(pl.multiple_of(n * 16, 16), 16)
        both = jnp.swapaxes(wi[rows].astype(F32), 0, 1)
        wd[:, rows, :] = both.astype(BF16)
        return carry

    lax.fori_loop(0, 64, pairs, 0)
    for n in range(4):
        wh[64 * n : 64 * n + 64, :] = wb[64 * (n // 2) : 64 * (n // 2) + 64, :]
    steps = wst[...].astype(F32)
    for h in range(4):
        wh[256 + 64 * h : 320 + 64 * h, :] = jnp.broadcast_to(steps[0, h : h + 1, :], (64, 1024)).astype(BF16)
        wv[64 * h : 64 * h + 64, :] = jnp.broadcast_to(steps[1, h : h + 1, :], (64, 1024)).astype(BF16)

    whole(0, zb).wait_recv()
    row = zb[...].astype(F32)
    xr[hd] = jnp.concatenate(
        [row[:, 0:8, :].reshape(64, 128), row[:, 8:16, :].reshape(64, 128)], axis=1
    ).astype(BF16)
    for p in x_peers:
        send(2, xr.at[hd], xr.at[hd], (gr, gc, p))

    whole(1, xt).wait_recv()
    gate = jnp.zeros((64, 256), F32)
    bcv = jnp.zeros((64, 128), F32)
    raw = jnp.zeros((64, 256), F32)
    for f in range(4):
        part, at = xt[f], slice(256 * f, 256 * f + 256)
        gate = gate + nn(part, wd[1, at, :])
        bcv = bcv + nt(part, wb[128:256, at])
        raw = raw + nt(part, wv[:, at])
    vstep = jax.nn.softplus(raw + by_head([bias[1, h] for h in range(4)], (64, 256)))
    gate = jax.nn.silu(gate) * gain[...]
    for c in range(8):
        at = slice(8 * c, 8 * c + 8)
        for half in range(2):
            lanes = slice(128 * half, 128 * half + 128)
            es[2 * c + half, :, 0:128] = gate[at, lanes]
            es[2 * c + half, :, 128:256] = bcv[at, :]
            es[2 * c + half, :, 256:384] = vstep[at, lanes]
    eb[gr] = es[gr]
    for p in y_peers:
        send(3, es.at[p], eb.at[gr], (p, gc, hd))

    whole(2, xr).wait_recv()
    uvals = jnp.zeros((64, 256), F32)
    proj = jnp.zeros((64, 512), F32)
    for f in range(4):
        part, at = xr[f], slice(256 * f, 256 * f + 256)
        uvals = uvals + nn(part, wd[0, at, :])
        proj = proj + nt(part, wh[:, at])
    hstep = jax.nn.softplus(proj[:, 256:512] + by_head([bias[0, h] for h in range(4)], (64, 256)))
    sums = segment_sums(hstep * by_head([-decay[0, h] for h in range(4)], (64, 256)), 64, 4)
    scores = dots(proj[:, 128:256], proj[:, 0:128], 4)
    i, lane = iotas((64, 256))
    mixing = jnp.where(i >= lane % 64, scores * jnp.exp(sums), 0.0)
    k, lane = iotas((256, 256))
    x_high, x_low = (
        jnp.where(k // 64 == lane // 64, jnp.concatenate([part] * 4, axis=0), jnp.zeros((), BF16))
        for part in split(hstep * uvals)
    )
    high, low = split(mixing)
    yh = nn(high, x_high) + nn(low, x_high) + nn(high, x_low)
    yh = yh + uvals * by_head([skip[h] for h in range(4)], (64, 256))
    def eight(n):
        return pl.ds(pl.multiple_of(n * 8, 8), 8)

    for half in range(2):
        yhz[half] = yh[:, 128 * half : 128 * half + 128]
        yhb[half, eight(gc), :] = yhz[half, eight(gc), :]
    for p in z_peers:
        send(4, yhz.at[:, eight(p), :], yhb.at[:, eight(gc), :], (gr, p, hd))

    for p in x_peers:
        send(5, columns(p), woc.at[hd], (gr, gc, p))

    whole(3, eb).wait_recv()
    ready = eb[...].reshape(128, 384)
    vdt = ready[:, 256:384]
    rates = jnp.concatenate(
        [
            jnp.broadcast_to(vdt[:, 64 * h : 64 * h + 1] * -decay[1, 2 * core + h], (128, 128))
            for h in range(2)
        ],
        axis=1,
    )
    sums = segment_sums(rates, 128, 2)
    bmat, cmat = (jnp.concatenate([ready[:, at : at + 64]] * 2, axis=1) for at in (128, 192))
    scores = dots(cmat, bmat, 2)
    i, lane = iotas((128, 256))
    high, low = split(jnp.where(i >= lane % 128, scores * jnp.exp(sums), 0.0))
    mix[:, 0:256] = high
    mix[:, 256:512] = low

    whole(4, yhb).wait_recv()
    for c in range(8):
        for half in range(2):
            ys[2 * c + half] = yhb[half, pl.ds(c, 8, stride=8), :]
    yb[gr] = ys[gr]
    for p in y_peers:
        send(6, ys.at[p], yb.at[gr], (p, gc, hd))

    whole(0, zb).wait_send()
    whole(1, xt).wait_send()
    whole(2, xr).wait_send()
    whole(3, eb).wait_send()
    whole(4, yhb).wait_send()
    whole(5, woc).wait_send()

    whole(6, yb).wait_recv()
    yh = yb[...].reshape(128, 128)
    k, lane = iotas((128, 128))
    zero = jnp.zeros((), BF16)
    x_high, x_low = (
        jnp.concatenate([jnp.where(lane < 64, part, zero), jnp.where(lane >= 64, part, zero)], axis=0)
        for part in split(eb[...].reshape(128, 384)[:, 256:384] * yh)
    )
    yv = nn(mix[:, 0:256], x_high) + nn(mix[:, 256:512], x_high) + nn(mix[:, 0:256], x_low) + yh
    high, low = split(yv * yv)
    k, lane = iotas((256, 128))
    same = jnp.where((k % 128) // 64 == lane // 64, 1.0, 0.0).astype(BF16)
    meansq = nn(jnp.concatenate([high, low], axis=1), same) * (1.0 / 64.0)
    hidden = yv * lax.rsqrt(meansq + 1e-05) * eb[...].reshape(128, 384)[:, 0:128]
    hs[...] = hidden.astype(BF16).astype(F32).reshape(16, 8, 128)
    hb[gr] = hs[gr]
    for p in y_peers:
        send(7, hs.at[p], hb.at[gr], (p, gc, hd))
    whole(6, yb).wait_send()

    whole(7, hb).wait_recv()
    for c in range(8):
        for half in range(2):
            ot[half, pl.ds(c, 8, stride=8), :] = hb[2 * c + half]
    hx[hd] = jnp.concatenate([ot[0], ot[1]], axis=1).astype(BF16)
    for p in x_peers:
        send(8, hx.at[hd], hx.at[hd], (gr, gc, p))
    whole(7, hb).wait_send()
    whole(5, woc).wait_recv()
    whole(8, hx).wait_recv()
    mixed = jnp.zeros((64, 256), F32)
    for f in range(4):
        mixed = mixed + nn(hx[f], woc[f])
    out[...] = mixed.astype(BF16)
    whole(8, hx).wait_send()


def on_device(patches, w_in, w_bc, w_step, step_bias, decay_rate, skip_gain, norm_gain, w_out):
    hbm, vmem, smem = (pl.BlockSpec(memory_space=m) for m in (pltpu.HBM, pltpu.VMEM, pltpu.SMEM))
    scratch = [
        pltpu.VMEM((8, 8, 256), BF16),
        pltpu.VMEM((8, 16, 128), BF16),
        pltpu.VMEM((8, 16, 128), BF16),
        pltpu.VMEM((4, 64, 256), BF16),
        pltpu.VMEM((4, 64, 256), BF16),
        pltpu.VMEM((1024, 2, 256), BF16),
        pltpu.VMEM((2, 1024, 256), BF16),
        pltpu.VMEM((256, 1024), BF16),
        pltpu.VMEM((2, 4, 1024), BF16),
        pltpu.VMEM((512, 1024), BF16),
        pltpu.VMEM((256, 1024), BF16),
        pltpu.VMEM((4, 256, 256), BF16),
        pltpu.VMEM((1, 256), F32),
        pltpu.SMEM((2, 4), F32),
        pltpu.SMEM((2, 4), F32),
        pltpu.SMEM((4,), F32),
        pltpu.VMEM((2, 64, 128), F32),
        pltpu.VMEM((2, 64, 128), F32),
        pltpu.VMEM((16, 8, 384), F32),
        pltpu.VMEM((16, 8, 384), F32),
        pltpu.VMEM((16, 8, 128), F32),
        pltpu.VMEM((16, 8, 128), F32),
        pltpu.VMEM((16, 8, 128), F32),
        pltpu.VMEM((16, 8, 128), F32),
        pltpu.VMEM((4, 64, 256), BF16),
        pltpu.VMEM((2, 64, 128), F32),
        pltpu.VMEM((128, 512), BF16),
        pltpu.SemaphoreType.DMA((9,)),
        pltpu.SemaphoreType.DMA((9,)),
        pltpu.SemaphoreType.DMA((9,)),
    ]
    mixed = pl.pallas_call(
        layer,
        out_shape=jax.ShapeDtypeStruct((64, 256), BF16),
        in_specs=[hbm] * 9,
        out_specs=vmem,
        scratch_shapes=scratch,
        compiler_params=pltpu.CompilerParams(
            collective_id=0, has_side_effects=True, vmem_limit_bytes=60 * 2**20
        ),
    )(
        patches,
        w_in,
        w_bc.transpose(1, 2, 0).reshape(256, 1024),
        w_step.transpose(1, 2, 0),
        step_bias,
        decay_rate,
        skip_gain,
        norm_gain.reshape(1, 256),
        w_out,
    )
    return mixed.reshape(8, 8, 256)


def solution(mesh):
    in_specs = (
        P("gr", "gc", "hd"),
        P(None, None, "hd"),
        P(),
        P(None, None, "hd"),
        P(None, "hd"),
        P(None, "hd"),
        P("hd"),
        P("hd"),
        P("hd", None),
    )
    out_specs = P("gr", "gc", "hd")
    return jax.shard_map(
        on_device, mesh=mesh, in_specs=in_specs, out_specs=out_specs, check_vma=False
    )
```

time: 307 us -> 44.6 us (0.15)
  waiting for transfers between devices: 180 us -> 0 us
  blocking collectives: 52.6 us -> 0 us
  Pallas kernels: 0 us -> 43 us
  other arithmetic: 39.2 us -> 0 us
  between operations: 13.3 us -> 0.01 us
  matrix products: 12.4 us -> 0 us
  local copies, waits for them, and re-layouts: 6.1 us -> 1.38 us
    all_gather x2 -> x0, waiting for transfers between devices: 157 us -> none  [carried_in(): everything = jax.tree.map(lambda part: lax.all_gather(part, axis), shard)]
    all_gather x3 -> x0, blocking collectives: 52.6 us -> none  [the longest x2 42.1 us: carried_in(): everything = jax.tree.map(lambda part: lax.all_gather(part, axis), shard)]
    pallas_call x0 -> x1, Pallas kernels: none -> 43 us  [on_device(): pl.pallas_call(layer, out_shape=jax.ShapeDtypeStruct((64, 256), BF16), in...]
    select_n x24 -> x0, other arithmetic: 35 us -> none  [step(): return jax.tree.map(lambda a, b: jnp.where(reached, a, b), new, before)]
    reduce_scatter x1 -> x0, waiting for transfers between devices: 22.4 us -> none  [on_device(): lax.psum_scatter(partial_out, 'hd', scatter_dimension=2, tiled=True)]
    dot_general x12 -> x0, matrix products: 12.4 us -> none  [the longest x2 5.84 us: tile_terms(): jnp.einsum('ajh,ajn,ajhp->ahnp', tail, bmat, inputs, precision=lax.Precis...]
  transfers between devices with their start and end apart: 3 -> 0, of which waited for: 3 -> 0; matrix products, arithmetic and copies ran while one was open for 1% -> 0% of each run, Pallas kernels for 0% -> 0%
where the time goes in v1:
time: 44.6 us; the launch traced here: 44.4 us
  Pallas kernels  43 us (96%)
  local copies, waits for them, and re-layouts  1.38 us (3%)
    pallas_call x1, Pallas kernels, on_device(): pl.pallas_call(layer, out_shape=jax.ShapeDtypeStruct((64, 256), BF16), in...  43 us
    unnamed x1, local copies, waits for them, and re-layouts  1.38 us

profile of v1, /device:TPU:1, one launch (start us, length us, event | category | flops | bytes accessed | tf_op | source)
XLA Modules:
  0.0 44.4 jit_solution(12371935336047792011)
XLA Ops:
  0.0 43.0 %shard_map.91 = bf16[64,256]{1,0:T(8,128)(2,1)} custom-call(bf16[8,8,256]{2,1,0:T(8,128)(2,1)} %patches.1, bf16[1024,2,256]{2,1,0:T(2,128)(2,1)} %w_in.1, bf16[256,1024]{1,0:T(8,128)(2,1)} %bitcast.6, bf16[2,4,1024]{2,1,0:T(4,128)(2,1)} %bitcast.8, f32[2,4]{1,0:T(2,128)} %bias_in.1, f32[2,4]{1,0:T(2,128)} %decay_in.1, f32[4]{0:T(128)} %skip_in.1, ...), custom_call_target="tpu_custom_call" | custom-call | tf_op jit(solution)/shard_map/pallas_call | solution.py:328
  43.0 1.4 %copy.11 = bf16[8,8,256]{2,1,0:T(8,128)(2,1)} copy(bf16[8,8,256]{2,1,0:T(8,128)(2,1)} %bitcast.7) | data formatting | bytes 65536

commit v2 on v1

--- a/solution.py
+++ b/solution.py
@@ -59,7 +59,7 @@
 def layer(
     patches, w_in, w_bc, w_step, bias_in, decay_in, skip_in, gain_in, w_out, out,
     pt, zs, zb, xr, xt, wi, wd, wb, wst, wh, wv, woc, gain, bias, decay, skip,
-    yhz, yhb, es, eb, ys, yb, hs, hb, hx, ot, mix,
+    yhz, yhb, es, eb, ys, yb, hs, hx, ot, mix,
     load_sem, send_sem, recv_sem,
 ):
     gr, gc, hd = lax.axis_index("gr"), lax.axis_index("gc"), lax.axis_index("hd")
@@ -268,27 +268,27 @@
     same = jnp.where((k % 128) // 64 == lane // 64, 1.0, 0.0).astype(BF16)
     meansq = nn(jnp.concatenate([high, low], axis=1), same) * (1.0 / 64.0)
     hidden = yv * lax.rsqrt(meansq + 1e-05) * eb[...].reshape(128, 384)[:, 0:128]
-    hs[...] = hidden.astype(BF16).astype(F32).reshape(16, 8, 128)
-    hb[gr] = hs[gr]
-    for p in y_peers:
-        send(7, hs.at[p], hb.at[gr], (p, gc, hd))
+    hs[...] = hidden.reshape(16, 8, 128).astype(BF16)
+
+    slot = (2 * hd + core) * 8 + chip
+    hx[slot] = hs[gr]
+    for p in y_peers + [gr]:
+        for q in x_peers + [hd]:
+            if not (p is gr and q is hd):
+                send(7, hs.at[p], hx.at[slot], (p, gc, q))
     whole(6, yb).wait_send()
-
-    whole(7, hb).wait_recv()
-    for c in range(8):
-        for half in range(2):
-            ot[half, pl.ds(c, 8, stride=8), :] = hb[2 * c + half]
-    hx[hd] = jnp.concatenate([ot[0], ot[1]], axis=1).astype(BF16)
-    for p in x_peers:
-        send(8, hx.at[hd], hx.at[hd], (gr, gc, p))
-    whole(7, hb).wait_send()
     whole(5, woc).wait_recv()
-    whole(8, hx).wait_recv()
+
+    whole(7, hx).wait_recv()
     mixed = jnp.zeros((64, 256), F32)
     for f in range(4):
-        mixed = mixed + nn(hx[f], woc[f])
-    out[...] = mixed.astype(BF16)
-    whole(8, hx).wait_send()
+        part = [hx[at : at + 8].astype(F32).reshape(64, 128) for at in (16 * f, 16 * f + 8)]
+        mixed = mixed + nn(jnp.concatenate(part, axis=1).astype(BF16), woc[f])
+    for c in range(8):
+        for half in range(2):
+            ot[half, pl.ds(c, 8, stride=8), :] = mixed[8 * c : 8 * c + 8, 128 * half : 128 * half + 128]
+    out[...] = jnp.concatenate([ot[0], ot[1]], axis=1).astype(BF16)
+    whole(7, hx).wait_send()
 
 
 def on_device(patches, w_in, w_bc, w_step, step_bias, decay_rate, skip_gain, norm_gain, w_out):
@@ -316,14 +316,13 @@
         pltpu.VMEM((16, 8, 384), F32),
         pltpu.VMEM((16, 8, 128), F32),
         pltpu.VMEM((16, 8, 128), F32),
-        pltpu.VMEM((16, 8, 128), F32),
-        pltpu.VMEM((16, 8, 128), F32),
-        pltpu.VMEM((4, 64, 256), BF16),
+        pltpu.VMEM((16, 8, 128), BF16),
+        pltpu.VMEM((64, 8, 128), BF16),
         pltpu.VMEM((2, 64, 128), F32),
         pltpu.VMEM((128, 512), BF16),
         pltpu.SemaphoreType.DMA((9,)),
-        pltpu.SemaphoreType.DMA((9,)),
-        pltpu.SemaphoreType.DMA((9,)),
+        pltpu.SemaphoreType.DMA((8,)),
+        pltpu.SemaphoreType.DMA((8,)),
     ]
     mixed = pl.pallas_call(
         layer,

time: 44.6 us -> 43.4 us (0.973)
  Pallas kernels: 43 us -> 41.8 us
    pallas_call x1, Pallas kernels: 43 us -> 41.8 us  [on_device(): pl.pallas_call(layer, out_shape=jax.ShapeDtypeStruct((64, 256), BF16), in...]
where the time goes in v2:
time: 43.4 us; the launch traced here: 43.2 us
  Pallas kernels  41.8 us (96%)
  local copies, waits for them, and re-layouts  1.38 us (3%)
    pallas_call x1, Pallas kernels, on_device(): pl.pallas_call(layer, out_shape=jax.ShapeDtypeStruct((64, 256), BF16), in...  41.8 us
    unnamed x1, local copies, waits for them, and re-layouts  1.38 us

profile of v2, /device:TPU:1, one launch (start us, length us, event | category | flops | bytes accessed | tf_op | source)
XLA Modules:
  0.0 43.2 jit_solution(6607640170257883934)
XLA Ops:
  0.0 41.8 %shard_map.91 = bf16[64,256]{1,0:T(8,128)(2,1)} custom-call(bf16[8,8,256]{2,1,0:T(8,128)(2,1)} %patches.1, bf16[1024,2,256]{2,1,0:T(2,128)(2,1)} %w_in.1, bf16[256,1024]{1,0:T(8,128)(2,1)} %bitcast.6, bf16[2,4,1024]{2,1,0:T(4,128)(2,1)} %bitcast.8, f32[2,4]{1,0:T(2,128)} %bias_in.1, f32[2,4]{1,0:T(2,128)} %decay_in.1, f32[4]{0:T(128)} %skip_in.1, ...), custom_call_target="tpu_custom_call" | custom-call | tf_op jit(solution)/shard_map/pallas_call | solution.py:327
  41.8 1.4 %copy.11 = bf16[8,8,256]{2,1,0:T(8,128)(2,1)} copy(bf16[8,8,256]{2,1,0:T(8,128)(2,1)} %bitcast.7) | data formatting | bytes 65536

commit v3 on v2

--- a/solution.py
+++ b/solution.py
@@ -11,6 +11,10 @@
 F32, BF16 = jnp.float32, jnp.bfloat16
 FAR_FIRST_8 = (4, 3, 5, 2, 6, 1, 7)
 FAR_FIRST_4 = (2, 1, 3)
+
+
+def abs_hops(k):
+    return min(k, 8 - k)
 
 
 def nn(a, b):
@@ -59,7 +63,7 @@
 def layer(
     patches, w_in, w_bc, w_step, bias_in, decay_in, skip_in, gain_in, w_out, out,
     pt, zs, zb, xr, xt, wi, wd, wb, wst, wh, wv, woc, gain, bias, decay, skip,
-    yhz, yhb, es, eb, ys, yb, hs, hx, ot, mix,
+    yhz, es, eb, yb, hs, hx, ot, mix,
     load_sem, send_sem, recv_sem,
 ):
     gr, gc, hd = lax.axis_index("gr"), lax.axis_index("gc"), lax.axis_index("hd")
@@ -69,6 +73,13 @@
     z_peers = [lax.rem(gc + k, 8) for k in FAR_FIRST_8]
     y_peers = [2 * lax.rem(chip + k, 8) + c for k in FAR_FIRST_8 for c in (core, 1 - core)]
     y_peers.append(2 * chip + 1 - core)
+
+    plane = [
+        (far + abs_hops(k), p, q)
+        for far, p in zip((4, 4, 3, 3, 3, 3, 2, 2, 2, 2, 1, 1, 1, 1, 0, 0), y_peers + [gr])
+        for k, q in zip(FAR_FIRST_8 + (0,), z_peers + [gc])
+    ]
+    plane = [(p, q) for _, p, q in sorted(plane[:-1], key=lambda entry: -entry[0])]
 
     barrier = pltpu.get_barrier_semaphore()
     for p in z_peers:
@@ -111,7 +122,7 @@
         ).start()
 
     def whole(phase, buf):
-        part = buf.at[:, pl.ds(0, 56), :] if phase == 4 else buf.at[pl.ds(0, buf.shape[0] - 1)]
+        part = buf.at[pl.ds(0, buf.shape[0] - 1)]
         return pltpu.make_async_remote_copy(
             src_ref=part,
             dst_ref=part,
@@ -209,14 +220,12 @@
     high, low = split(mixing)
     yh = nn(high, x_high) + nn(low, x_high) + nn(high, x_low)
     yh = yh + uvals * by_head([skip[h] for h in range(4)], (64, 256))
-    def eight(n):
-        return pl.ds(pl.multiple_of(n * 8, 8), 8)
-
     for half in range(2):
         yhz[half] = yh[:, 128 * half : 128 * half + 128]
-        yhb[half, eight(gc), :] = yhz[half, eight(gc), :]
-    for p in z_peers:
-        send(4, yhz.at[:, eight(p), :], yhb.at[:, eight(gc), :], (gr, p, hd))
+    mine = 8 * gr + gc
+    yb[pl.ds(mine, 1), :] = yhz[core, pl.ds(8 * gc + chip, 1), :]
+    for p, q in plane:
+        send(4, yhz.at[lax.rem(p, 2), pl.ds(8 * q + lax.div(p, 2), 1), :], yb.at[pl.ds(mine, 1), :], (p, q, hd))
 
     for p in x_peers:
         send(5, columns(p), woc.at[hd], (gr, gc, p))
@@ -239,23 +248,15 @@
     mix[:, 0:256] = high
     mix[:, 256:512] = low
 
-    whole(4, yhb).wait_recv()
-    for c in range(8):
-        for half in range(2):
-            ys[2 * c + half] = yhb[half, pl.ds(c, 8, stride=8), :]
-    yb[gr] = ys[gr]
-    for p in y_peers:
-        send(6, ys.at[p], yb.at[gr], (p, gc, hd))
-
     whole(0, zb).wait_send()
     whole(1, xt).wait_send()
     whole(2, xr).wait_send()
     whole(3, eb).wait_send()
-    whole(4, yhb).wait_send()
+    whole(4, yb).wait_send()
     whole(5, woc).wait_send()
 
-    whole(6, yb).wait_recv()
-    yh = yb[...].reshape(128, 128)
+    whole(4, yb).wait_recv()
+    yh = yb[...]
     k, lane = iotas((128, 128))
     zero = jnp.zeros((), BF16)
     x_high, x_low = (
@@ -276,7 +277,6 @@
         for q in x_peers + [hd]:
             if not (p is gr and q is hd):
                 send(7, hs.at[p], hx.at[slot], (p, gc, q))
-    whole(6, yb).wait_send()
     whole(5, woc).wait_recv()
 
     whole(7, hx).wait_recv()
@@ -311,11 +311,9 @@
         pltpu.SMEM((2, 4), F32),
         pltpu.SMEM((4,), F32),
         pltpu.VMEM((2, 64, 128), F32),
-        pltpu.VMEM((2, 64, 128), F32),
         pltpu.VMEM((16, 8, 384), F32),
         pltpu.VMEM((16, 8, 384), F32),
-        pltpu.VMEM((16, 8, 128), F32),
-        pltpu.VMEM((16, 8, 128), F32),
+        pltpu.VMEM((128, 128), F32),
         pltpu.VMEM((16, 8, 128), BF16),
         pltpu.VMEM((64, 8, 128), BF16),
         pltpu.VMEM((2, 64, 128), F32),

time: 43.4 us -> 40.7 us (0.938)
  Pallas kernels: 41.8 us -> 39.1 us
    pallas_call x1, Pallas kernels: 41.8 us -> 39.1 us  [on_device(): pl.pallas_call(layer, out_shape=jax.ShapeDtypeStruct((64, 256), BF16), in...]
where the time goes in v3:
time: 40.7 us; the launch traced here: 40.5 us
  Pallas kernels  39.1 us (96%)
  local copies, waits for them, and re-layouts  1.38 us (3%)
    pallas_call x1, Pallas kernels, on_device(): pl.pallas_call(layer, out_shape=jax.ShapeDtypeStruct((64, 256), BF16), in...  39.1 us
    unnamed x1, local copies, waits for them, and re-layouts  1.38 us

profile of v3, /device:TPU:1, one launch (start us, length us, event | category | flops | bytes accessed | tf_op | source)
XLA Modules:
  0.0 40.5 jit_solution(604409070547391085)
XLA Ops:
  0.0 39.1 %shard_map.91 = bf16[64,256]{1,0:T(8,128)(2,1)} custom-call(bf16[8,8,256]{2,1,0:T(8,128)(2,1)} %patches.1, bf16[1024,2,256]{2,1,0:T(2,128)(2,1)} %w_in.1, bf16[256,1024]{1,0:T(8,128)(2,1)} %bitcast.6, bf16[2,4,1024]{2,1,0:T(4,128)(2,1)} %bitcast.8, f32[2,4]{1,0:T(2,128)} %bias_in.1, f32[2,4]{1,0:T(2,128)} %decay_in.1, f32[4]{0:T(128)} %skip_in.1, ...), custom_call_target="tpu_custom_call" | custom-call | tf_op jit(solution)/shard_map/pallas_call | solution.py:325
  39.1 1.4 %copy.11 = bf16[8,8,256]{2,1,0:T(8,128)(2,1)} copy(bf16[8,8,256]{2,1,0:T(8,128)(2,1)} %bitcast.7) | data formatting | bytes 65536

commit v4 on v3

--- a/solution.py
+++ b/solution.py
@@ -11,10 +11,6 @@
 F32, BF16 = jnp.float32, jnp.bfloat16
 FAR_FIRST_8 = (4, 3, 5, 2, 6, 1, 7)
 FAR_FIRST_4 = (2, 1, 3)
-
-
-def abs_hops(k):
-    return min(k, 8 - k)
 
 
 def nn(a, b):
@@ -51,35 +47,60 @@
     return nt(jnp.concatenate(left, axis=1), jnp.concatenate([right] * copies, axis=0))
 
 
-def segment_sums(rates, length, heads):
+def reaches(later, earlier, rows):
+    return (later >= earlier) & (later % rows == earlier % rows)
+
+
+def ones_where(mask):
+    return jnp.where(mask, 1.0, 0.0).astype(BF16)
+
+
+def segment_sums(rates, length, heads, rows):
     k, lane = iotas((length, heads * length))
-    inside = jnp.where(k > lane % length, rates, 0.0)
-    high, low = split(inside)
-    i, j = iotas((length, 2 * length))
-    lower = jnp.where(i >= j % length, 1.0, 0.0).astype(BF16)
-    return nn(lower, jnp.concatenate([high, low], axis=0))
+    j = lane % length
+    inside = split(jnp.where(reaches(k, j, rows) & (k != j), rates, 0.0))
+    i, k = iotas((length, 2 * length))
+    return nn(ones_where(reaches(i, k % length, rows)), jnp.concatenate(inside, axis=0))
+
+
+def sums_across(rates, before):
+    k, lane = iotas((64, 256))
+    j = lane % 64
+    after = jnp.where(reaches(k, j, 2) & (k != j), before, 0.0)
+    parts = split(jnp.concatenate([rates, after], axis=0))
+    i, k = iotas((64, 256))
+    return nn(ones_where((k % 128 >= 64) | reaches(i, k % 64, 2)), jnp.concatenate(parts, axis=0))
+
+
+def head_blocks(x):
+    k, lane = iotas((256, 256))
+    zero = jnp.zeros((), BF16)
+    return [
+        jnp.where(k // 64 == lane // 64, jnp.concatenate([part] * 4, axis=0), zero) for part in split(x)
+    ]
+
+
+def mixed_by(mixing, x):
+    high, low = split(mixing)
+    x_high, x_low = head_blocks(x)
+    return nn(high, x_high) + nn(low, x_high) + nn(high, x_low)
 
 
 def layer(
     patches, w_in, w_bc, w_step, bias_in, decay_in, skip_in, gain_in, w_out, out,
-    pt, zs, zb, xr, xt, wi, wd, wb, wst, wh, wv, woc, gain, bias, decay, skip,
+    pt, zs, xr, xl, xt, wi, wd, wb, wst, wh, wv, woc, gain, bias, decay, skip,
     yhz, es, eb, yb, hs, hx, ot, mix,
-    load_sem, send_sem, recv_sem,
+    load_sem, send_sem, recv_sem, ready,
 ):
     gr, gc, hd = lax.axis_index("gr"), lax.axis_index("gc"), lax.axis_index("hd")
     chip, core = lax.div(gr, 2), lax.rem(gr, 2)
 
+    side, quarter = lax.div(gc, 4), lax.rem(gc, 4)
+
     x_peers = [lax.rem(hd + k, 4) for k in FAR_FIRST_4]
-    z_peers = [lax.rem(gc + k, 8) for k in FAR_FIRST_8]
+    z_peers = [4 * side + lax.rem(quarter + k, 4) for k in FAR_FIRST_4]
     y_peers = [2 * lax.rem(chip + k, 8) + c for k in FAR_FIRST_8 for c in (core, 1 - core)]
     y_peers.append(2 * chip + 1 - core)
-
-    plane = [
-        (far + abs_hops(k), p, q)
-        for far, p in zip((4, 4, 3, 3, 3, 3, 2, 2, 2, 2, 1, 1, 1, 1, 0, 0), y_peers + [gr])
-        for k, q in zip(FAR_FIRST_8 + (0,), z_peers + [gc])
-    ]
-    plane = [(p, q) for _, p, q in sorted(plane[:-1], key=lambda entry: -entry[0])]
 
     barrier = pltpu.get_barrier_semaphore()
     for p in z_peers:
@@ -88,6 +109,11 @@
         pl.semaphore_signal(barrier, inc=1, device_id=(p, gc, hd), device_id_type=MESH)
     for p in x_peers:
         pl.semaphore_signal(barrier, inc=1, device_id=(gr, gc, p), device_id_type=MESH)
+
+    @pl.when(side == 0)
+    def _():
+        for p in range(4, 8):
+            pl.semaphore_signal(barrier, inc=1, device_id=(gr, p, hd), device_id_type=MESH)
 
     def columns(p):
         return w_out.at[:, pl.ds(pl.multiple_of(p * 256, 256), 256)]
@@ -121,8 +147,7 @@
             device_id_type=MESH,
         ).start()
 
-    def whole(phase, buf):
-        part = buf.at[pl.ds(0, buf.shape[0] - 1)]
+    def done(phase, part):
         return pltpu.make_async_remote_copy(
             src_ref=part,
             dst_ref=part,
@@ -132,24 +157,32 @@
             device_id_type=MESH,
         )
 
+    def but_one(buf):
+        return buf.at[pl.ds(0, buf.shape[0] - 1)]
+
+    def sixteen(n):
+        return pl.ds(pl.multiple_of(n * 16, 16), 16)
+
     loads[0].wait()
     tile = pt[...].astype(F32)
     for r in range(8):
-        zs[r] = jnp.concatenate([tile[r, :, 0:128], tile[r, :, 128:256]], axis=0).astype(BF16)
         for half in range(2):
-            ot[half, 8 * r : 8 * r + 8, :] = tile[r, :, 128 * half : 128 * half + 128]
-    for c in range(0, 8, 2):
-        for half in range(2):
-            pair = [ot[half, pl.ds(c + d, 8, stride=8), :] for d in (0, 1)]
-            xt[hd, 8 * c : 8 * c + 16, 128 * half : 128 * half + 128] = jnp.concatenate(
-                pair, axis=0
-            ).astype(BF16)
-    zb[gc] = zs[gc]
-
-    pl.semaphore_wait(barrier, 25)
+            lanes = tile[r, :, 128 * half : 128 * half + 128]
+            ot[half, pl.ds(r, 8, stride=8), :] = lanes
+            yhz[half, pl.ds(16 * (r // 2) + r % 2, 8, stride=2), :] = lanes
+    xt[hd] = jnp.concatenate([ot[0], ot[1]], axis=1).astype(BF16)
+    zs[...] = jnp.concatenate([yhz[0], yhz[1]], axis=1).astype(BF16)
+    xr[hd, sixteen(quarter), :] = zs[sixteen(quarter), :]
+
+    pl.semaphore_wait(barrier, 21 + 4 * side)
+
+    @pl.when(side == 1)
+    def _():
+        for p in range(4):
+            pl.semaphore_signal(ready, inc=1, device_id=(gr, p, hd), device_id_type=MESH)
 
     for p in z_peers:
-        send(0, zs.at[p], zb.at[gc], (gr, p, hd))
+        send(0, zs.at[sixteen(lax.rem(p, 4)), :], xr.at[hd, sixteen(quarter), :], (gr, p, hd))
     for p in x_peers:
         send(1, xt.at[hd], xt.at[hd], (gr, gc, p))
 
@@ -170,15 +203,17 @@
         wh[256 + 64 * h : 320 + 64 * h, :] = jnp.broadcast_to(steps[0, h : h + 1, :], (64, 1024)).astype(BF16)
         wv[64 * h : 64 * h + 64, :] = jnp.broadcast_to(steps[1, h : h + 1, :], (64, 1024)).astype(BF16)
 
-    whole(0, zb).wait_recv()
-    row = zb[...].astype(F32)
-    xr[hd] = jnp.concatenate(
-        [row[:, 0:8, :].reshape(64, 128), row[:, 8:16, :].reshape(64, 128)], axis=1
-    ).astype(BF16)
+    done(0, xr.at[0, pl.ds(0, 48), :]).wait_recv()
     for p in x_peers:
         send(2, xr.at[hd], xr.at[hd], (gr, gc, p))
 
-    whole(1, xt).wait_recv()
+    @pl.when(side == 0)
+    def _():
+        pl.semaphore_wait(ready, 4)
+        for p in range(4):
+            send(6, zs.at[sixteen(p), :], xl.at[hd, sixteen(quarter), :], (gr, 4 + p, hd))
+
+    done(1, but_one(xt)).wait_recv()
     gate = jnp.zeros((64, 256), F32)
     bcv = jnp.zeros((64, 128), F32)
     raw = jnp.zeros((64, 256), F32)
@@ -200,37 +235,57 @@
     for p in y_peers:
         send(3, es.at[p], eb.at[gr], (p, gc, hd))
 
-    whole(2, xr).wait_recv()
-    uvals = jnp.zeros((64, 256), F32)
-    proj = jnp.zeros((64, 512), F32)
-    for f in range(4):
-        part, at = xr[f], slice(256 * f, 256 * f + 256)
-        uvals = uvals + nn(part, wd[0, at, :])
-        proj = proj + nt(part, wh[:, at])
-    hstep = jax.nn.softplus(proj[:, 256:512] + by_head([bias[0, h] for h in range(4)], (64, 256)))
-    sums = segment_sums(hstep * by_head([-decay[0, h] for h in range(4)], (64, 256)), 64, 4)
-    scores = dots(proj[:, 128:256], proj[:, 0:128], 4)
+    @pl.when(side == 1)
+    def _():
+        done(6, xl.at[0]).wait_recv()
+        for p in x_peers:
+            send(8, xl.at[hd], xl.at[hd], (gr, gc, p))
+
+    def project(patch):
+        uvals = jnp.zeros((64, 256), F32)
+        proj = jnp.zeros((64, 512), F32)
+        for f in range(4):
+            part, at = patch[f], slice(256 * f, 256 * f + 256)
+            uvals = uvals + nn(part, wd[0, at, :])
+            proj = proj + nt(part, wh[:, at])
+        steps = jax.nn.softplus(proj[:, 256:512] + by_head([bias[0, h] for h in range(4)], (64, 256)))
+        rates = steps * by_head([-decay[0, h] for h in range(4)], (64, 256))
+        return uvals, proj[:, 0:128], proj[:, 128:256], rates, steps * uvals
+
+    done(2, but_one(xr)).wait_recv()
+    uvals, bmat, cmat, rates, xin = project(xr)
     i, lane = iotas((64, 256))
-    mixing = jnp.where(i >= lane % 64, scores * jnp.exp(sums), 0.0)
-    k, lane = iotas((256, 256))
-    x_high, x_low = (
-        jnp.where(k // 64 == lane // 64, jnp.concatenate([part] * 4, axis=0), jnp.zeros((), BF16))
-        for part in split(hstep * uvals)
-    )
-    high, low = split(mixing)
-    yh = nn(high, x_high) + nn(low, x_high) + nn(high, x_low)
+    mixing = dots(cmat, bmat, 4) * jnp.exp(segment_sums(rates, 64, 4, 2))
+    yh = mixed_by(jnp.where(reaches(i, lane % 64, 2), mixing, 0.0), xin)
     yh = yh + uvals * by_head([skip[h] for h in range(4)], (64, 256))
     for half in range(2):
         yhz[half] = yh[:, 128 * half : 128 * half + 128]
-    mine = 8 * gr + gc
-    yb[pl.ds(mine, 1), :] = yhz[core, pl.ds(8 * gc + chip, 1), :]
-    for p, q in plane:
-        send(4, yhz.at[lax.rem(p, 2), pl.ds(8 * q + lax.div(p, 2), 1), :], yb.at[pl.ds(mine, 1), :], (p, q, hd))
+
+    @pl.when(side == 1)
+    def _():
+        done(8, but_one(xl)).wait_recv()
+        _, b_left, _, rates_left, x_left = project(xl)
+        mixing = dots(cmat, b_left, 4) * jnp.exp(sums_across(rates, rates_left))
+        more = mixed_by(jnp.where(i % 2 == lane % 2, mixing, 0.0), x_left)
+        for half in range(2):
+            yhz[half] = yhz[half] + more[:, 128 * half : 128 * half + 128]
+
+    def pair(n):
+        return pl.ds(pl.multiple_of(n * 2, 2), 2)
+
+    mine = 4 * gr + quarter
+    for r in range(2):
+        yb[pl.ds(2 * mine + r, 1), :] = yhz[core, pl.ds(2 * (8 * quarter + chip) + r, 1), :]
+    for p in y_peers + [gr]:
+        for q in z_peers + [gc]:
+            if not (p is gr and q is gc):
+                column = 8 * lax.rem(q, 4) + lax.div(p, 2)
+                send(4, yhz.at[lax.rem(p, 2), pair(column), :], yb.at[pair(mine), :], (p, q, hd))
 
     for p in x_peers:
         send(5, columns(p), woc.at[hd], (gr, gc, p))
 
-    whole(3, eb).wait_recv()
+    done(3, but_one(eb)).wait_recv()
     ready = eb[...].reshape(128, 384)
     vdt = ready[:, 256:384]
     rates = jnp.concatenate(
@@ -240,7 +295,7 @@
         ],
         axis=1,
     )
-    sums = segment_sums(rates, 128, 2)
+    sums = segment_sums(rates, 128, 2, 1)
     bmat, cmat = (jnp.concatenate([ready[:, at : at + 64]] * 2, axis=1) for at in (128, 192))
     scores = dots(cmat, bmat, 2)
     i, lane = iotas((128, 256))
@@ -248,14 +303,21 @@
     mix[:, 0:256] = high
     mix[:, 256:512] = low
 
-    whole(0, zb).wait_send()
-    whole(1, xt).wait_send()
-    whole(2, xr).wait_send()
-    whole(3, eb).wait_send()
-    whole(4, yb).wait_send()
-    whole(5, woc).wait_send()
-
-    whole(4, yb).wait_recv()
+    done(0, xr.at[0, pl.ds(0, 48), :]).wait_send()
+    done(1, but_one(xt)).wait_send()
+    done(2, but_one(xr)).wait_send()
+    done(3, but_one(eb)).wait_send()
+    done(5, but_one(woc)).wait_send()
+
+    @pl.when(side == 0)
+    def _():
+        done(6, xl.at[0]).wait_send()
+
+    @pl.when(side == 1)
+    def _():
+        done(8, but_one(xl)).wait_send()
+
+    done(4, yb.at[pl.ds(0, 126)]).wait_recv()
     yh = yb[...]
     k, lane = iotas((128, 128))
     zero = jnp.zeros((), BF16)
@@ -277,9 +339,10 @@
         for q in x_peers + [hd]:
             if not (p is gr and q is hd):
                 send(7, hs.at[p], hx.at[slot], (p, gc, q))
-    whole(5, woc).wait_recv()
-
-    whole(7, hx).wait_recv()
+    done(4, yb.at[pl.ds(0, 126)]).wait_send()
+    done(5, but_one(woc)).wait_recv()
+
+    done(7, but_one(hx)).wait_recv()
     mixed = jnp.zeros((64, 256), F32)
     for f in range(4):
         part = [hx[at : at + 8].astype(F32).reshape(64, 128) for at in (16 * f, 16 * f + 8)]
@@ -288,15 +351,15 @@
         for half in range(2):
             ot[half, pl.ds(c, 8, stride=8), :] = mixed[8 * c : 8 * c + 8, 128 * half : 128 * half + 128]
     out[...] = jnp.concatenate([ot[0], ot[1]], axis=1).astype(BF16)
-    whole(7, hx).wait_send()
+    done(7, but_one(hx)).wait_send()
 
 
 def on_device(patches, w_in, w_bc, w_step, step_bias, decay_rate, skip_gain, norm_gain, w_out):
     hbm, vmem, smem = (pl.BlockSpec(memory_space=m) for m in (pltpu.HBM, pltpu.VMEM, pltpu.SMEM))
     scratch = [
         pltpu.VMEM((8, 8, 256), BF16),
-        pltpu.VMEM((8, 16, 128), BF16),
-        pltpu.VMEM((8, 16, 128), BF16),
+        pltpu.VMEM((64, 256), BF16),
+        pltpu.VMEM((4, 64, 256), BF16),
         pltpu.VMEM((4, 64, 256), BF16),
         pltpu.VMEM((4, 64, 256), BF16),
         pltpu.VMEM((1024, 2, 256), BF16),
@@ -319,12 +382,13 @@
         pltpu.VMEM((2, 64, 128), F32),
         pltpu.VMEM((128, 512), BF16),
         pltpu.SemaphoreType.DMA((9,)),
-        pltpu.SemaphoreType.DMA((8,)),
-        pltpu.SemaphoreType.DMA((8,)),
+        pltpu.SemaphoreType.DMA((9,)),
+        pltpu.SemaphoreType.DMA((9,)),
+        pltpu.SemaphoreType.REGULAR,
     ]
     mixed = pl.pallas_call(
         layer,
-        out_shape=jax.ShapeDtypeStruct((64, 256), BF16),
+        out_shape=pltpu.VMEM((64, 256), BF16),
         in_specs=[hbm] * 9,
         out_specs=vmem,
         scratch_shapes=scratch,

time: 40.7 us -> 37.6 us (0.924)
  Pallas kernels: 39.1 us -> 36.8 us
  local copies, waits for them, and re-layouts: 1.38 us -> 0.62 us
    pallas_call x1, Pallas kernels: 39.1 us -> 36.8 us  [on_device(): pl.pallas_call(layer, out_shape=pltpu.VMEM((64, 256), BF16), in_specs=[hb...]
    unnamed x1, local copies, waits for them, and re-layouts: 1.38 us -> 0.62 us
where the time goes in v4:
time: 37.6 us; the launch traced here: 37.4 us
  Pallas kernels  36.8 us (98%)
  local copies, waits for them, and re-layouts  0.62 us (2%)
    pallas_call x1, Pallas kernels, on_device(): pl.pallas_call(layer, out_shape=pltpu.VMEM((64, 256), BF16), in_specs=[hb...  36.8 us

profile of v4, /device:TPU:1, one launch (start us, length us, event | category | flops | bytes accessed | tf_op | source)
XLA Modules:
  0.0 37.4 jit_solution(14788342152571419176)
XLA Ops:
  0.0 36.8 %shard_map.91 = bf16[64,256]{1,0:T(8,128)(2,1)S(1)} custom-call(bf16[8,8,256]{2,1,0:T(8,128)(2,1)} %patches.1, bf16[1024,2,256]{2,1,0:T(2,128)(2,1)} %w_in.1, bf16[256,1024]{1,0:T(8,128)(2,1)} %bitcast.7, bf16[2,4,1024]{2,1,0:T(4,128)(2,1)} %bitcast.8, f32[2,4]{1,0:T(2,128)} %bias_in.1, f32[2,4]{1,0:T(2,128)} %decay_in.1, f32[4]{0:T(128)} %skip_in.1, ...), custom_call_target="tpu_custom_call" | custom-call | tf_op jit(solution)/shard_map/pallas_call | solution.py:389
  36.8 0.6 %copy.11 = bf16[8,8,256]{2,1,0:T(8,128)(2,1)} copy(bf16[8,8,256]{2,1,0:T(8,128)(2,1)S(1)} %bitcast.6) | data formatting | bytes 65536

commit v5 on v4

--- a/solution.py
+++ b/solution.py
@@ -206,12 +206,6 @@
     done(0, xr.at[0, pl.ds(0, 48), :]).wait_recv()
     for p in x_peers:
         send(2, xr.at[hd], xr.at[hd], (gr, gc, p))
-
-    @pl.when(side == 0)
-    def _():
-        pl.semaphore_wait(ready, 4)
-        for p in range(4):
-            send(6, zs.at[sixteen(p), :], xl.at[hd, sixteen(quarter), :], (gr, 4 + p, hd))
 
     done(1, but_one(xt)).wait_recv()
     gate = jnp.zeros((64, 256), F32)
@@ -234,6 +228,12 @@
     eb[gr] = es[gr]
     for p in y_peers:
         send(3, es.at[p], eb.at[gr], (p, gc, hd))
+
+    @pl.when(side == 0)
+    def _():
+        pl.semaphore_wait(ready, 4)
+        for p in range(4):
+            send(6, zs.at[sixteen(p), :], xl.at[hd, sixteen(quarter), :], (gr, 4 + p, hd))
 
     @pl.when(side == 1)
     def _():

time: 37.6 us -> 35.4 us (0.941)
  the two profiles are of different devices: /device:TPU:1 before, /device:TPU:257 now
where the time goes in v5:
time: 35.4 us; the launch traced here: 35.2 us
  Pallas kernels  34.6 us (98%)
  local copies, waits for them, and re-layouts  0.62 us (2%)
    pallas_call x1, Pallas kernels, on_device(): pl.pallas_call(layer, out_shape=pltpu.VMEM((64, 256), BF16), in_specs=[hb...  34.6 us

profile of v5, /device:TPU:257, one launch (start us, length us, event | category | flops | bytes accessed | tf_op | source)
XLA Modules:
  0.0 35.2 jit_solution(14662006309875654773)
XLA Ops:
  0.0 34.6 %shard_map.91 = bf16[64,256]{1,0:T(8,128)(2,1)S(1)} custom-call(bf16[8,8,256]{2,1,0:T(8,128)(2,1)} %patches.1, bf16[1024,2,256]{2,1,0:T(2,128)(2,1)} %w_in.1, bf16[256,1024]{1,0:T(8,128)(2,1)} %bitcast.7, bf16[2,4,1024]{2,1,0:T(4,128)(2,1)} %bitcast.8, f32[2,4]{1,0:T(2,128)} %bias_in.1, f32[2,4]{1,0:T(2,128)} %decay_in.1, f32[4]{0:T(128)} %skip_in.1, ...), custom_call_target="tpu_custom_call" | custom-call | tf_op jit(solution)/shard_map/pallas_call | solution.py:389
  34.6 0.6 %copy.11 = bf16[8,8,256]{2,1,0:T(8,128)(2,1)} copy(bf16[8,8,256]{2,1,0:T(8,128)(2,1)S(1)} %bitcast.6) | data formatting | bytes 65536

commit v6 on v5

--- a/solution.py
+++ b/solution.py
@@ -83,14 +83,14 @@
 def mixed_by(mixing, x):
     high, low = split(mixing)
     x_high, x_low = head_blocks(x)
-    return nn(high, x_high) + nn(low, x_high) + nn(high, x_low)
+    return nn(jnp.concatenate([high, low, high], axis=1), jnp.concatenate([x_high, x_high, x_low], axis=0))
 
 
 def layer(
     patches, w_in, w_bc, w_step, bias_in, decay_in, skip_in, gain_in, w_out, out,
     pt, zs, xr, xl, xt, wi, wd, wb, wst, wh, wv, woc, gain, bias, decay, skip,
     yhz, es, eb, yb, hs, hx, ot, mix,
-    load_sem, send_sem, recv_sem, ready,
+    load_sem, send_sem, recv_sem, left_sem, ready,
 ):
     gr, gc, hd = lax.axis_index("gr"), lax.axis_index("gc"), lax.axis_index("hd")
     chip, core = lax.div(gr, 2), lax.rem(gr, 2)
@@ -137,22 +137,22 @@
     for load in loads:
         load.start()
 
-    def send(phase, src, dst, device):
+    def send(phase, src, dst, device, arrival=None):
         pltpu.make_async_remote_copy(
             src_ref=src,
             dst_ref=dst,
             send_sem=send_sem.at[phase],
-            recv_sem=recv_sem.at[phase],
+            recv_sem=recv_sem.at[phase] if arrival is None else arrival,
             device_id=device,
             device_id_type=MESH,
         ).start()
 
-    def done(phase, part):
+    def done(phase, part, arrival=None):
         return pltpu.make_async_remote_copy(
             src_ref=part,
             dst_ref=part,
             send_sem=send_sem.at[phase],
-            recv_sem=recv_sem.at[phase],
+            recv_sem=recv_sem.at[phase] if arrival is None else arrival,
             device_id=(gr, gc, x_peers[0]),
             device_id_type=MESH,
         )
@@ -208,14 +208,10 @@
         send(2, xr.at[hd], xr.at[hd], (gr, gc, p))
 
     done(1, but_one(xt)).wait_recv()
-    gate = jnp.zeros((64, 256), F32)
-    bcv = jnp.zeros((64, 128), F32)
-    raw = jnp.zeros((64, 256), F32)
-    for f in range(4):
-        part, at = xt[f], slice(256 * f, 256 * f + 256)
-        gate = gate + nn(part, wd[1, at, :])
-        bcv = bcv + nt(part, wb[128:256, at])
-        raw = raw + nt(part, wv[:, at])
+    features = jnp.concatenate([xt[f] for f in range(4)], axis=1)
+    gate = nn(features, wd[1])
+    bcv = nt(features, wb[128:256, :])
+    raw = nt(features, wv[...])
     vstep = jax.nn.softplus(raw + by_head([bias[1, h] for h in range(4)], (64, 256)))
     gate = jax.nn.silu(gate) * gain[...]
     for c in range(8):
@@ -233,27 +229,27 @@
     def _():
         pl.semaphore_wait(ready, 4)
         for p in range(4):
-            send(6, zs.at[sixteen(p), :], xl.at[hd, sixteen(quarter), :], (gr, 4 + p, hd))
+            send(6, zs.at[sixteen(p), :], xl.at[hd, sixteen(quarter), :], (gr, 4 + p, hd), left_sem.at[quarter])
 
     @pl.when(side == 1)
     def _():
-        done(6, xl.at[0]).wait_recv()
-        for p in x_peers:
-            send(8, xl.at[hd], xl.at[hd], (gr, gc, p))
+        for k in range(4):
+            n = jnp.where(quarter < 2, 3 - k, k)
+            done(6, xl.at[hd, sixteen(n), :], left_sem.at[n]).wait_recv()
+            for p in x_peers:
+                send(8, xl.at[hd, sixteen(n), :], xl.at[hd, sixteen(n), :], (gr, gc, p))
 
     def project(patch):
-        uvals = jnp.zeros((64, 256), F32)
-        proj = jnp.zeros((64, 512), F32)
-        for f in range(4):
-            part, at = patch[f], slice(256 * f, 256 * f + 256)
-            uvals = uvals + nn(part, wd[0, at, :])
-            proj = proj + nt(part, wh[:, at])
-        steps = jax.nn.softplus(proj[:, 256:512] + by_head([bias[0, h] for h in range(4)], (64, 256)))
+        features = jnp.concatenate([patch[f] for f in range(4)], axis=1)
+        uvals = nn(features, wd[0])
+        steps = nt(features, wh[256:512, :]) + by_head([bias[0, h] for h in range(4)], (64, 256))
+        steps = jax.nn.softplus(steps)
         rates = steps * by_head([-decay[0, h] for h in range(4)], (64, 256))
-        return uvals, proj[:, 0:128], proj[:, 128:256], rates, steps * uvals
+        return features, uvals, nt(features, wh[0:128, :]), rates, steps * uvals
 
     done(2, but_one(xr)).wait_recv()
-    uvals, bmat, cmat, rates, xin = project(xr)
+    features, uvals, bmat, rates, xin = project(xr)
+    cmat = nt(features, wh[128:256, :])
     i, lane = iotas((64, 256))
     mixing = dots(cmat, bmat, 4) * jnp.exp(segment_sums(rates, 64, 4, 2))
     yh = mixed_by(jnp.where(reaches(i, lane % 64, 2), mixing, 0.0), xin)
@@ -264,7 +260,7 @@
     @pl.when(side == 1)
     def _():
         done(8, but_one(xl)).wait_recv()
-        _, b_left, _, rates_left, x_left = project(xl)
+        _, _, b_left, rates_left, x_left = project(xl)
         mixing = dots(cmat, b_left, 4) * jnp.exp(sums_across(rates, rates_left))
         more = mixed_by(jnp.where(i % 2 == lane % 2, mixing, 0.0), x_left)
         for half in range(2):
@@ -302,6 +298,7 @@
     high, low = split(jnp.where(i >= lane % 128, scores * jnp.exp(sums), 0.0))
     mix[:, 0:256] = high
     mix[:, 256:512] = low
+    mix[:, 512:768] = high
 
     done(0, xr.at[0, pl.ds(0, 48), :]).wait_send()
     done(1, but_one(xt)).wait_send()
@@ -325,7 +322,7 @@
         jnp.concatenate([jnp.where(lane < 64, part, zero), jnp.where(lane >= 64, part, zero)], axis=0)
         for part in split(eb[...].reshape(128, 384)[:, 256:384] * yh)
     )
-    yv = nn(mix[:, 0:256], x_high) + nn(mix[:, 256:512], x_high) + nn(mix[:, 0:256], x_low) + yh
+    yv = nn(mix[...], jnp.concatenate([x_high, x_high, x_low], axis=0)) + yh
     high, low = split(yv * yv)
     k, lane = iotas((256, 128))
     same = jnp.where((k % 128) // 64 == lane // 64, 1.0, 0.0).astype(BF16)
@@ -343,10 +340,8 @@
     done(5, but_one(woc)).wait_recv()
 
     done(7, but_one(hx)).wait_recv()
-    mixed = jnp.zeros((64, 256), F32)
-    for f in range(4):
-        part = [hx[at : at + 8].astype(F32).reshape(64, 128) for at in (16 * f, 16 * f + 8)]
-        mixed = mixed + nn(jnp.concatenate(part, axis=1).astype(BF16), woc[f])
+    part = [hx[8 * n : 8 * n + 8].astype(F32).reshape(64, 128).astype(BF16) for n in range(8)]
+    mixed = nn(jnp.concatenate(part, axis=1), woc[...].reshape(1024, 256))
     for c in range(8):
         for half in range(2):
             ot[half, pl.ds(c, 8, stride=8), :] = mixed[8 * c : 8 * c + 8, 128 * half : 128 * half + 128]
@@ -380,10 +375,11 @@
         pltpu.VMEM((16, 8, 128), BF16),
         pltpu.VMEM((64, 8, 128), BF16),
         pltpu.VMEM((2, 64, 128), F32),
-        pltpu.VMEM((128, 512), BF16),
+        pltpu.VMEM((128, 768), BF16),
         pltpu.SemaphoreType.DMA((9,)),
         pltpu.SemaphoreType.DMA((9,)),
         pltpu.SemaphoreType.DMA((9,)),
+        pltpu.SemaphoreType.DMA((4,)),
         pltpu.SemaphoreType.REGULAR,
     ]
     mixed = pl.pallas_call(

time: 35.4 us -> 35 us (0.989)
  the two profiles are of different devices: /device:TPU:257 before, /device:TPU:1 now
where the time goes in v6:
time: 35 us; the launch traced here: 34.8 us
  Pallas kernels  34.2 us (98%)
  local copies, waits for them, and re-layouts  0.62 us (2%)
    pallas_call x1, Pallas kernels, on_device(): pl.pallas_call(layer, out_shape=pltpu.VMEM((64, 256), BF16), in_specs=[hb...  34.2 us

profile of v6, /device:TPU:1, one launch (start us, length us, event | category | flops | bytes accessed | tf_op | source)
XLA Modules:
  0.0 34.8 jit_solution(7655867329467803316)
XLA Ops:
  0.0 34.2 %shard_map.91 = bf16[64,256]{1,0:T(8,128)(2,1)S(1)} custom-call(bf16[8,8,256]{2,1,0:T(8,128)(2,1)} %patches.1, bf16[1024,2,256]{2,1,0:T(2,128)(2,1)} %w_in.1, bf16[256,1024]{1,0:T(8,128)(2,1)} %bitcast.7, bf16[2,4,1024]{2,1,0:T(4,128)(2,1)} %bitcast.8, f32[2,4]{1,0:T(2,128)} %bias_in.1, f32[2,4]{1,0:T(2,128)} %decay_in.1, f32[4]{0:T(128)} %skip_in.1, ...), custom_call_target="tpu_custom_call" | custom-call | tf_op jit(solution)/shard_map/pallas_call | solution.py:385
  34.2 0.6 %copy.11 = bf16[8,8,256]{2,1,0:T(8,128)(2,1)} copy(bf16[8,8,256]{2,1,0:T(8,128)(2,1)S(1)} %bitcast.6) | data formatting | bytes 65536

commit v7 on v6

--- a/solution.py
+++ b/solution.py
@@ -89,7 +89,7 @@
 def layer(
     patches, w_in, w_bc, w_step, bias_in, decay_in, skip_in, gain_in, w_out, out,
     pt, zs, xr, xl, xt, wi, wd, wb, wst, wh, wv, woc, gain, bias, decay, skip,
-    yhz, es, eb, yb, hs, hx, ot, mix,
+    yhz, es, eb, gs, gb, yb, hs, hx, ot, mix,
     load_sem, send_sem, recv_sem, left_sem, ready,
 ):
     gr, gc, hd = lax.axis_index("gr"), lax.axis_index("gc"), lax.axis_index("hd")
@@ -103,10 +103,10 @@
     y_peers.append(2 * chip + 1 - core)
 
     barrier = pltpu.get_barrier_semaphore()
+    for p in y_peers:
+        pl.semaphore_signal(barrier, inc=1, device_id=(p, gc, hd), device_id_type=MESH)
     for p in z_peers:
         pl.semaphore_signal(barrier, inc=1, device_id=(gr, p, hd), device_id_type=MESH)
-    for p in y_peers:
-        pl.semaphore_signal(barrier, inc=1, device_id=(p, gc, hd), device_id_type=MESH)
     for p in x_peers:
         pl.semaphore_signal(barrier, inc=1, device_id=(gr, gc, p), device_id_type=MESH)
 
@@ -218,10 +218,11 @@
         at = slice(8 * c, 8 * c + 8)
         for half in range(2):
             lanes = slice(128 * half, 128 * half + 128)
-            es[2 * c + half, :, 0:128] = gate[at, lanes]
-            es[2 * c + half, :, 128:256] = bcv[at, :]
-            es[2 * c + half, :, 256:384] = vstep[at, lanes]
+            es[2 * c + half, :, 0:128] = bcv[at, :]
+            es[2 * c + half, :, 128:256] = vstep[at, lanes]
+            gs[2 * c + half] = gate[at, lanes]
     eb[gr] = es[gr]
+    gb[gr] = gs[gr]
     for p in y_peers:
         send(3, es.at[p], eb.at[gr], (p, gc, hd))
 
@@ -278,12 +279,15 @@
                 column = 8 * lax.rem(q, 4) + lax.div(p, 2)
                 send(4, yhz.at[lax.rem(p, 2), pair(column), :], yb.at[pair(mine), :], (p, q, hd))
 
+    for p in y_peers:
+        send(9, gs.at[p], gb.at[gr], (p, gc, hd))
+
     for p in x_peers:
         send(5, columns(p), woc.at[hd], (gr, gc, p))
 
     done(3, but_one(eb)).wait_recv()
-    ready = eb[...].reshape(128, 384)
-    vdt = ready[:, 256:384]
+    ready = eb[...].reshape(128, 256)
+    vdt = ready[:, 128:256]
     rates = jnp.concatenate(
         [
             jnp.broadcast_to(vdt[:, 64 * h : 64 * h + 1] * -decay[1, 2 * core + h], (128, 128))
@@ -292,7 +296,7 @@
         axis=1,
     )
     sums = segment_sums(rates, 128, 2, 1)
-    bmat, cmat = (jnp.concatenate([ready[:, at : at + 64]] * 2, axis=1) for at in (128, 192))
+    bmat, cmat = (jnp.concatenate([ready[:, at : at + 64]] * 2, axis=1) for at in (0, 64))
     scores = dots(cmat, bmat, 2)
     i, lane = iotas((128, 256))
     high, low = split(jnp.where(i >= lane % 128, scores * jnp.exp(sums), 0.0))
@@ -304,6 +308,7 @@
     done(1, but_one(xt)).wait_send()
     done(2, but_one(xr)).wait_send()
     done(3, but_one(eb)).wait_send()
+    done(9, but_one(gb)).wait_send()
     done(5, but_one(woc)).wait_send()
 
     @pl.when(side == 0)
@@ -320,22 +325,23 @@
     zero = jnp.zeros((), BF16)
     x_high, x_low = (
         jnp.concatenate([jnp.where(lane < 64, part, zero), jnp.where(lane >= 64, part, zero)], axis=0)
-        for part in split(eb[...].reshape(128, 384)[:, 256:384] * yh)
+        for part in split(eb[...].reshape(128, 256)[:, 128:256] * yh)
     )
     yv = nn(mix[...], jnp.concatenate([x_high, x_high, x_low], axis=0)) + yh
     high, low = split(yv * yv)
     k, lane = iotas((256, 128))
-    same = jnp.where((k % 128) // 64 == lane // 64, 1.0, 0.0).astype(BF16)
+    same = ones_where((k % 128) // 64 == lane // 64)
     meansq = nn(jnp.concatenate([high, low], axis=1), same) * (1.0 / 64.0)
-    hidden = yv * lax.rsqrt(meansq + 1e-05) * eb[...].reshape(128, 384)[:, 0:128]
+    done(9, but_one(gb)).wait_recv()
+    hidden = yv * lax.rsqrt(meansq + 1e-05) * gb[...].reshape(128, 128)
     hs[...] = hidden.reshape(16, 8, 128).astype(BF16)
 
     slot = (2 * hd + core) * 8 + chip
     hx[slot] = hs[gr]
-    for p in y_peers + [gr]:
-        for q in x_peers + [hd]:
-            if not (p is gr and q is hd):
-                send(7, hs.at[p], hx.at[slot], (p, gc, q))
+    far = zip((4, 4, 3, 3, 3, 3, 2, 2, 2, 2, 1, 1, 1, 1, 0, 0), y_peers + [gr])
+    holders = [(m + n, p, q) for m, p in far for n, q in zip((2, 1, 1, 0), x_peers + [hd])]
+    for _, p, q in sorted(holders[:-1], key=lambda entry: -entry[0]):
+        send(7, hs.at[p], hx.at[slot], (p, gc, q))
     done(4, yb.at[pl.ds(0, 126)]).wait_send()
     done(5, but_one(woc)).wait_recv()
 
@@ -369,16 +375,18 @@
         pltpu.SMEM((2, 4), F32),
         pltpu.SMEM((4,), F32),
         pltpu.VMEM((2, 64, 128), F32),
-        pltpu.VMEM((16, 8, 384), F32),
-        pltpu.VMEM((16, 8, 384), F32),
+        pltpu.VMEM((16, 8, 256), F32),
+        pltpu.VMEM((16, 8, 256), F32),
+        pltpu.VMEM((16, 8, 128), F32),
+        pltpu.VMEM((16, 8, 128), F32),
         pltpu.VMEM((128, 128), F32),
         pltpu.VMEM((16, 8, 128), BF16),
         pltpu.VMEM((64, 8, 128), BF16),
         pltpu.VMEM((2, 64, 128), F32),
         pltpu.VMEM((128, 768), BF16),
-        pltpu.SemaphoreType.DMA((9,)),
-        pltpu.SemaphoreType.DMA((9,)),
-        pltpu.SemaphoreType.DMA((9,)),
+        pltpu.SemaphoreType.DMA((10,)),
+        pltpu.SemaphoreType.DMA((10,)),
+        pltpu.SemaphoreType.DMA((10,)),
         pltpu.SemaphoreType.DMA((4,)),
         pltpu.SemaphoreType.REGULAR,
     ]

time: 35 us -> 34.6 us (0.989)
  Pallas kernels: 34.2 us -> 33.6 us
    pallas_call x1, Pallas kernels: 34.2 us -> 33.6 us  [on_device(): pl.pallas_call(layer, out_shape=pltpu.VMEM((64, 256), BF16), in_specs=[hb...]
where the time goes in v7:
time: 34.6 us; the launch traced here: 34.2 us
  Pallas kernels  33.6 us (97%)
  local copies, waits for them, and re-layouts  0.62 us (2%)
    pallas_call x1, Pallas kernels, on_device(): pl.pallas_call(layer, out_shape=pltpu.VMEM((64, 256), BF16), in_specs=[hb...  33.6 us

profile of v7, /device:TPU:1, one launch (start us, length us, event | category | flops | bytes accessed | tf_op | source)
XLA Modules:
  0.0 34.2 jit_solution(202783963492064011)
XLA Ops:
  0.0 33.6 %shard_map.91 = bf16[64,256]{1,0:T(8,128)(2,1)S(1)} custom-call(bf16[8,8,256]{2,1,0:T(8,128)(2,1)} %patches.1, bf16[1024,2,256]{2,1,0:T(2,128)(2,1)} %w_in.1, bf16[256,1024]{1,0:T(8,128)(2,1)} %bitcast.7, bf16[2,4,1024]{2,1,0:T(4,128)(2,1)} %bitcast.8, f32[2,4]{1,0:T(2,128)} %bias_in.1, f32[2,4]{1,0:T(2,128)} %decay_in.1, f32[4]{0:T(128)} %skip_in.1, ...), custom_call_target="tpu_custom_call" | custom-call | tf_op jit(solution)/shard_map/pallas_call | solution.py:393
  33.6 0.6 %copy.11 = bf16[8,8,256]{2,1,0:T(8,128)(2,1)} copy(bf16[8,8,256]{2,1,0:T(8,128)(2,1)S(1)} %bitcast.6) | data formatting | bytes 65536

commit v8 on v7

--- a/solution.py
+++ b/solution.py
@@ -240,16 +240,26 @@
             for p in x_peers:
                 send(8, xl.at[hd, sixteen(n), :], xl.at[hd, sixteen(n), :], (gr, gc, p))
 
-    def project(patch):
-        features = jnp.concatenate([patch[f] for f in range(4)], axis=1)
-        uvals = nn(features, wd[0])
-        steps = nt(features, wh[256:512, :]) + by_head([bias[0, h] for h in range(4)], (64, 256))
+    def terms(uvals, steps, bmat):
+        steps = steps + by_head([bias[0, h] for h in range(4)], (64, 256))
         steps = jax.nn.softplus(steps)
         rates = steps * by_head([-decay[0, h] for h in range(4)], (64, 256))
-        return features, uvals, nt(features, wh[0:128, :]), rates, steps * uvals
+        return uvals, bmat, rates, steps * uvals
+
+    def block_products(blocks):
+        at = [pl.ds(pl.multiple_of(256 * f, 256), 256) for f in blocks]
+        part = jnp.concatenate([xl[f] for f in blocks], axis=1)
+        return (
+            nn(part, jnp.concatenate([wd[0, n, :] for n in at], axis=0)),
+            nt(part, jnp.concatenate([wh[256:512, n] for n in at], axis=1)),
+            nt(part, jnp.concatenate([wh[0:128, n] for n in at], axis=1)),
+        )
 
     done(2, but_one(xr)).wait_recv()
-    features, uvals, bmat, rates, xin = project(xr)
+    features = jnp.concatenate([xr[f] for f in range(4)], axis=1)
+    uvals, bmat, rates, xin = terms(
+        nn(features, wd[0]), nt(features, wh[256:512, :]), nt(features, wh[0:128, :])
+    )
     cmat = nt(features, wh[128:256, :])
     i, lane = iotas((64, 256))
     mixing = dots(cmat, bmat, 4) * jnp.exp(segment_sums(rates, 64, 4, 2))
@@ -260,8 +270,10 @@
 
     @pl.when(side == 1)
     def _():
+        own = block_products([hd])
         done(8, but_one(xl)).wait_recv()
-        _, _, b_left, rates_left, x_left = project(xl)
+        others = block_products(x_peers)
+        _, b_left, rates_left, x_left = terms(*[a + b for a, b in zip(own, others)])
         mixing = dots(cmat, b_left, 4) * jnp.exp(sums_across(rates, rates_left))
         more = mixed_by(jnp.where(i % 2 == lane % 2, mixing, 0.0), x_left)
         for half in range(2):

time: 34.6 us -> 34.7 us (level)
  no operation moved by 1% of the time
where the time goes in v8:
time: 34.7 us; the launch traced here: 34.2 us
  Pallas kernels  33.6 us (97%)
  local copies, waits for them, and re-layouts  0.62 us (2%)
    pallas_call x1, Pallas kernels, on_device(): pl.pallas_call(layer, out_shape=pltpu.VMEM((64, 256), BF16), in_specs=[hb...  33.6 us

profile of v8, /device:TPU:1, one launch (start us, length us, event | category | flops | bytes accessed | tf_op | source)
XLA Modules:
  0.0 34.2 jit_solution(4206312789944820685)
XLA Ops:
  0.0 33.6 %shard_map.91 = bf16[64,256]{1,0:T(8,128)(2,1)S(1)} custom-call(bf16[8,8,256]{2,1,0:T(8,128)(2,1)} %patches.1, bf16[1024,2,256]{2,1,0:T(2,128)(2,1)} %w_in.1, bf16[256,1024]{1,0:T(8,128)(2,1)} %bitcast.7, bf16[2,4,1024]{2,1,0:T(4,128)(2,1)} %bitcast.8, f32[2,4]{1,0:T(2,128)} %bias_in.1, f32[2,4]{1,0:T(2,128)} %decay_in.1, f32[4]{0:T(128)} %skip_in.1, ...), custom_call_target="tpu_custom_call" | custom-call | tf_op jit(solution)/shard_map/pallas_call | solution.py:405
  33.6 0.6 %copy.11 = bf16[8,8,256]{2,1,0:T(8,128)(2,1)} copy(bf16[8,8,256]{2,1,0:T(8,128)(2,1)S(1)} %bitcast.6) | data formatting | bytes 65536

commit v9 on v7

--- a/solution.py
+++ b/solution.py
@@ -178,7 +178,8 @@
 
     @pl.when(side == 1)
     def _():
-        for p in range(4):
+        for k in range(4):
+            p = jnp.where(quarter < 2, k, 3 - k)
             pl.semaphore_signal(ready, inc=1, device_id=(gr, p, hd), device_id_type=MESH)
 
     for p in z_peers:
@@ -229,7 +230,8 @@
     @pl.when(side == 0)
     def _():
         pl.semaphore_wait(ready, 4)
-        for p in range(4):
+        for k in range(4):
+            p = jnp.where(quarter < 2, k, 3 - k)
             send(6, zs.at[sixteen(p), :], xl.at[hd, sixteen(quarter), :], (gr, 4 + p, hd), left_sem.at[quarter])
 
     @pl.when(side == 1)

time: 34.6 us -> 34.6 us (level)
  no operation moved by 1% of the time
where the time goes in v9:
time: 34.6 us; the launch traced here: 34.2 us
  Pallas kernels  33.6 us (97%)
  local copies, waits for them, and re-layouts  0.62 us (2%)
    pallas_call x1, Pallas kernels, on_device(): pl.pallas_call(layer, out_shape=pltpu.VMEM((64, 256), BF16), in_specs=[hb...  33.6 us

profile of v9, /device:TPU:1, one launch (start us, length us, event | category | flops | bytes accessed | tf_op | source)
XLA Modules:
  0.0 34.2 jit_solution(349810503943826202)
XLA Ops:
  0.0 33.6 %shard_map.91 = bf16[64,256]{1,0:T(8,128)(2,1)S(1)} custom-call(bf16[8,8,256]{2,1,0:T(8,128)(2,1)} %patches.1, bf16[1024,2,256]{2,1,0:T(2,128)(2,1)} %w_in.1, bf16[256,1024]{1,0:T(8,128)(2,1)} %bitcast.7, bf16[2,4,1024]{2,1,0:T(4,128)(2,1)} %bitcast.8, f32[2,4]{1,0:T(2,128)} %bias_in.1, f32[2,4]{1,0:T(2,128)} %decay_in.1, f32[4]{0:T(128)} %skip_in.1, ...), custom_call_target="tpu_custom_call" | custom-call | tf_op jit(solution)/shard_map/pallas_call | solution.py:395
  33.6 0.6 %copy.11 = bf16[8,8,256]{2,1,0:T(8,128)(2,1)} copy(bf16[8,8,256]{2,1,0:T(8,128)(2,1)S(1)} %bitcast.6) | data formatting | bytes 65536
